TPU v7x, 256 devices: a whole 4x4x8 slice. The times are simulated.
256 devices in a mesh: ctx: 32 (over y_hi, z, core), dp: 8 (over y_lo, x).
Axes of the slice: x: 4, y: 4 (y_hi: 2, y_lo: 2; y = y_hi * 2 + y_lo), z: 8, core: 2. Of those that a mesh axis runs over, the one named last changes fastest.
Arguments:
- query_rows: bfloat16 [8, 8192, 512], P('dp', 'ctx'), may hold values from -25 to 25
- key_rows: bfloat16 [8, 8192, 512], P('dp', 'ctx'), may hold values from -25 to 25
- value_rows: bfloat16 [8, 8192, 512], P('dp', 'ctx'), may hold values from -20 to 20
- recordings: int32 [8, 32], P('dp'), may hold values from 0 to 3, never falling along the last dimension, each value on 1 to 11 neighbouring positions
- out_weight: bfloat16 [512, 1024], replicated, may hold values from -0.25 to 0.25
- cotangent: bfloat16 [8, 8192, 1024], P('dp', 'ctx'), may hold values from -12 to 12
Outputs:
- projected: bfloat16 [8, 8192, 1024], P('dp', 'ctx')
- grad_query: bfloat16 [8, 8192, 512], P('dp', 'ctx')
- grad_key: bfloat16 [8, 8192, 512], P('dp', 'ctx')
- grad_value: bfloat16 [8, 8192, 512], P('dp', 'ctx')
- grad_weight: bfloat16 [512, 1024], replicated
Inputs may be any that keep to these rules, and one draw needn't show every extreme that they name: `recordings`: along the blocks of a batch the ids never fall; each recording covers 1 to 11 consecutive blocks, and some covers exactly 11.
All inputs are finite; a program needn't handle non-finite values.
Results may differ from a plain program's by a relative error of at most 0.02.
Values may be sent and summed in bfloat16 or wider, within the bound.
A program may use at most 128 MiB of HBM per device.

v0:
```python
from functools import reduce
import math

import jax
import jax.numpy as jnp
from jax import lax
from jax.sharding import PartitionSpec as P

HEADS = 4
MOST = 11


def from_behind(value, axis, by):
    count = lax.axis_size(axis)
    pairs = [(i, i + by) for i in range(count) if 0 <= i + by < count]
    return lax.ppermute(value, axis, pairs)


def split_heads(matrix):
    return matrix.reshape(matrix.shape[0], HEADS, matrix.shape[1] // HEADS)


def block_scores(queries, key_heads, factor):
    return (
        jnp.einsum("qhe,khe->hqk", queries, key_heads, preferred_element_type=jnp.float32) * factor
    )


def absorb(softmax_state, queries, key_heads, value_heads, key_mask, factor):
    maxima, totals, summed = softmax_state
    scores = block_scores(queries, key_heads, factor)
    if key_mask is not None:
        scores = jnp.where(key_mask[None, None, :], scores, -jnp.inf)
    raised = jnp.maximum(maxima, jnp.max(scores, axis=-1))
    shrink = jnp.exp(maxima - raised)
    exp_terms = jnp.exp(scores - raised[:, :, None])
    weights = exp_terms.astype(jnp.bfloat16)
    totals = totals * shrink + jnp.sum(exp_terms, axis=-1)
    summed = summed * shrink.T[:, :, None] + jnp.einsum(
        "hqk,khe->qhe", weights, value_heads, preferred_element_type=jnp.float32
    )
    return (raised, totals, summed)


def query_term(
    query_grad, queries, grad_heads, log_totals, row_dots, key_heads, value_heads, key_mask, factor
):
    soft_probs = jnp.exp(block_scores(queries, key_heads, factor) - log_totals[:, :, None])
    if key_mask is not None:
        soft_probs = jnp.where(key_mask[None, None, :], soft_probs, 0.0)
    grad_probs = jnp.einsum(
        "qhe,khe->hqk", grad_heads, value_heads, preferred_element_type=jnp.float32
    )
    grad_scores = (soft_probs * (grad_probs - row_dots[:, :, None])).astype(jnp.bfloat16)
    return query_grad + jnp.einsum(
        "hqk,khe->qhe", grad_scores, key_heads, preferred_element_type=jnp.float32
    )


def key_term(
    key_grads, queries, grad_heads, log_totals, row_dots, key_heads, value_heads, query_mask, factor
):
    grad_keys, grad_values = key_grads
    soft_probs = jnp.exp(block_scores(queries, key_heads, factor) - log_totals[:, :, None])
    if query_mask is not None:
        soft_probs = jnp.where(query_mask[None, :, None], soft_probs, 0.0)
    grad_values = grad_values + jnp.einsum(
        "hqk,qhe->khe",
        soft_probs.astype(jnp.bfloat16),
        grad_heads,
        preferred_element_type=jnp.float32,
    )
    grad_probs = jnp.einsum(
        "qhe,khe->hqk", grad_heads, value_heads, preferred_element_type=jnp.float32
    )
    grad_scores = (soft_probs * (grad_probs - row_dots[:, :, None])).astype(jnp.bfloat16)
    grad_keys = grad_keys + jnp.einsum(
        "hqk,qhe->khe", grad_scores, queries, preferred_element_type=jnp.float32
    )
    return (grad_keys, grad_values)


def on_device(query_rows, key_rows, value_rows, recordings, out_weight, cotangent):
    tok_rows = query_rows.shape[1]
    att_width = query_rows.shape[2]
    head_size = att_width // HEADS
    factor = 1.0 / math.sqrt(head_size)
    queries = split_heads(query_rows[0])
    key_heads = split_heads(key_rows[0])
    value_heads = split_heads(value_rows[0])
    position = lax.axis_index("ctx")
    labels = recordings[0]
    block_ids = jnp.arange(labels.shape[0], dtype=jnp.int32)

    def label_of(source):
        return jnp.max(jnp.where(block_ids == source, labels, -1))

    own_label = label_of(position)

    def keep_same(current):
        return current

    def join_group(waiting, join_dims):
        members = tuple(
            (
                jnp.concatenate(
                    [element[0][member_id] for element in waiting], axis=join_dims[member_id]
                )
                for member_id in range(len(join_dims))
            )
        )
        matched = [label_of(element[1]) == own_label for element in waiting]
        row_mask = jnp.concatenate(
            [jnp.broadcast_to(flag_value, (tok_rows,)) for flag_value in matched]
        )
        any_valid = reduce(jnp.logical_or, matched)
        return (members, row_mask, any_valid)

    softmax_state = (
        jnp.full((HEADS, tok_rows), -jnp.inf, jnp.float32),
        jnp.zeros((HEADS, tok_rows), jnp.float32),
        jnp.zeros((tok_rows, HEADS, head_size), jnp.float32),
    )
    softmax_state = absorb(softmax_state, queries, key_heads, value_heads, None, factor)
    kept_groups = []

    def absorb_group(state, waiting):
        members, row_mask, any_valid = join_group(waiting, (0, 0))
        kept_groups.append((members, row_mask, any_valid))
        return lax.cond(
            any_valid,
            lambda current: absorb(current, queries, members[0], members[1], row_mask, factor),
            keep_same,
            state,
        )

    moving = (key_heads, value_heads)
    waiting = []
    for offset in range(1, MOST):
        moving = from_behind((moving[0], moving[1]), "ctx", 1)
        waiting.append((moving, position - offset))
        if len(waiting) == 2 or offset == MOST - 1:
            softmax_state = absorb_group(softmax_state, waiting)
            waiting = []
    moving = (key_heads, value_heads)
    waiting = []
    for offset in range(1, MOST):
        moving = from_behind((moving[0], moving[1]), "ctx", -1)
        waiting.append((moving, position + offset))
        if len(waiting) == 2 or offset == MOST - 1:
            softmax_state = absorb_group(softmax_state, waiting)
            waiting = []
    maxima, totals, summed = softmax_state
    attended = (summed / totals.T[:, :, None]).reshape(tok_rows, att_width).astype(jnp.bfloat16)
    log_totals = maxima + jnp.log(totals)
    projected = jnp.dot(attended, out_weight, preferred_element_type=jnp.float32).astype(
        jnp.bfloat16
    )
    grad_att = lax.dot_general(
        cotangent[0], out_weight, (((1,), (1,)), ((), ())), preferred_element_type=jnp.float32
    ).astype(jnp.bfloat16)
    row_dots = jnp.sum(
        (grad_att.astype(jnp.float32) * attended.astype(jnp.float32)).reshape(
            tok_rows, HEADS, head_size
        ),
        axis=-1,
    ).T
    grad_heads = split_heads(grad_att)
    empty_grad = jnp.zeros((tok_rows, HEADS, head_size), jnp.float32)
    query_grad = query_term(
        empty_grad, queries, grad_heads, log_totals, row_dots, key_heads, value_heads, None, factor
    )
    for members, row_mask, any_valid in kept_groups:
        query_grad = lax.cond(
            any_valid,
            lambda current: query_term(
                current,
                queries,
                grad_heads,
                log_totals,
                row_dots,
                members[0],
                members[1],
                row_mask,
                factor,
            ),
            keep_same,
            query_grad,
        )
    key_grads = key_term(
        (empty_grad, empty_grad),
        queries,
        grad_heads,
        log_totals,
        row_dots,
        key_heads,
        value_heads,
        None,
        factor,
    )

    def key_group(running, waiting):
        members, row_mask, any_valid = join_group(waiting, (0, 0, 1, 1))
        return lax.cond(
            any_valid,
            lambda current: key_term(
                current,
                members[0],
                members[1],
                members[2],
                members[3],
                key_heads,
                value_heads,
                row_mask,
                factor,
            ),
            keep_same,
            running,
        )

    package = (queries, grad_heads)
    statistics = (log_totals, row_dots)
    waiting = []
    for offset in range(1, MOST):
        package = from_behind((package[0], package[1]), "ctx", 1)
        statistics = from_behind((statistics[0], statistics[1]), "ctx", 1)
        waiting.append((package + statistics, position - offset))
        if len(waiting) == 2 or offset == MOST - 1:
            key_grads = key_group(key_grads, waiting)
            waiting = []
    package = (queries, grad_heads)
    statistics = (log_totals, row_dots)
    waiting = []
    for offset in range(1, MOST):
        package = from_behind((package[0], package[1]), "ctx", -1)
        statistics = from_behind((statistics[0], statistics[1]), "ctx", -1)
        waiting.append((package + statistics, position + offset))
        if len(waiting) == 2 or offset == MOST - 1:
            key_grads = key_group(key_grads, waiting)
            waiting = []
    weight_part = lax.dot_general(
        attended, cotangent[0], (((0,), (0,)), ((), ())), preferred_element_type=jnp.float32
    )
    summed_weight = lax.psum(weight_part, ("ctx", "dp"))
    all_rows = tok_rows * lax.axis_size("ctx") * lax.axis_size("dp")
    grad_weight = (summed_weight / math.sqrt(all_rows)).astype(jnp.bfloat16)
    grad_query = (query_grad * factor).reshape(tok_rows, att_width).astype(jnp.bfloat16)
    grad_key = (key_grads[0] * factor).reshape(tok_rows, att_width).astype(jnp.bfloat16)
    grad_value = key_grads[1].reshape(tok_rows, att_width).astype(jnp.bfloat16)
    return (projected[None], grad_query[None], grad_key[None], grad_value[None], grad_weight)


def solution(mesh):
    return jax.shard_map(
        on_device,
        mesh=mesh,
        in_specs=(
            P("dp", "ctx", None),
            P("dp", "ctx", None),
            P("dp", "ctx", None),
            P("dp", None),
            P(),
            P("dp", "ctx", None),
        ),
        out_specs=(
            P("dp", "ctx", None),
            P("dp", "ctx", None),
            P("dp", "ctx", None),
            P("dp", "ctx", None),
            P(),
        ),
        check_vma=False,
    )
```

profile of v0, /device:TPU:16, one launch (start us, length us, event | category | flops | bytes accessed | tf_op | source)
XLA Modules:
  0.0 787.1 jit_solution(11812326215813562762)
XLA Ops:
  10.3 7.3 collective-permute-start.20
  20.6 7.3 collective-permute-start.22
  100.6 7.3 collective-permute-start.24
  115.8 7.3 collective-permute-start.88
  156.0 7.3 collective-permute-start.28
  183.0 7.3 collective-permute-start.29
  224.2 7.3 collective-permute-start.34
  303.7 7.3 collective-permute-start.113
  423.6 7.3 collective-permute-start.83
  444.1 7.3 collective-permute-start.90
  464.5 7.3 collective-permute-start.91
  484.4 7.3 collective-permute-start.102
  527.1 7.3 collective-permute-start.99
  541.1 7.3 collective-permute-start.110
  550.4 7.3 collective-permute-start.93
  560.9 7.3 collective-permute-start.106
  583.7 7.3 collective-permute-start.107
  664.8 7.3 collective-permute-start.108
  710.2 18.4 %collective-permute-start.117 = (bf16[256,4,128]{0,2,1:T(8,128)(2,1)}, bf16[256,4,128]{0,2,1:T(8,128)(2,1)}, u32[]{:S(2)}, u32[]{:S(2)}) collective-permute-start(bf16[256,4,128]{0,2,1:T(8,128)(2,1)} %collective-permute-done.116), channel_id=1, source_target_pairs={{8,0},{16,8},{24,16},{32,24},{40,32},{48,40},{56,48},{64,56},{72,6... | collective-permute-start | bytes 786440 | tf_op jit(solution)/shard_map/ppermute | solution.py:16
  734.9 8.1 %conditional.55 = ((f32[256,4,128]{2,0,1:T(8,128)S(1)}, f32[256,4,128]{2,0,1:T(8,128)S(1)})) conditional(s32[]{:T(128)} %convert_element_type.255, (f32[256,4,128]{2,0,1:T(8,128)S(1)}, f32[256,4,128]{2,0,1:T(8,128)S(1)}) %get-tuple-element.2420, (pred[512]{0:T(512)(128)(4,1)S(1)}, bf16[512,4,128]{0,2,1:T(8,128)(2,1)}, ...), branch_computations={%region_94.95_spmd, %region_95.96_spmd} | conditional | flops 540803072 | bytes 11026968 | solution.py:204
  743.1 8.4 %conditional.56 = ((f32[256,4,128]{2,0,1:T(8,128)S(1)}, f32[256,4,128]{2,0,1:T(8,128)S(1)})) conditional(s32[]{:T(128)} %convert_element_type.254, (f32[256,4,128]{2,0,1:T(8,128)S(1)}, f32[256,4,128]{2,0,1:T(8,128)S(1)}) %get-tuple-element.2421, (pred[512]{0:T(512)(128)(4,1)S(1)}, bf16[512,4,128]{0,2,1:T(8,128)(2,1)}, ...), branch_computations={%region_96.97_spmd, %region_97.98_spmd} | conditional | flops 540803072 | bytes 13124148 | solution.py:204
  751.5 8.2 %conditional.57 = ((f32[256,4,128]{2,0,1:T(8,128)S(1)}, f32[256,4,128]{2,0,1:T(8,128)S(1)})) conditional(s32[]{:T(128)} %convert_element_type.253, (f32[256,4,128]{2,0,1:T(8,128)S(1)}, f32[256,4,128]{2,0,1:T(8,128)S(1)}) %get-tuple-element.2422, (pred[512]{0:T(512)(128)(4,1)S(1)}, bf16[512,4,128]{0,2,1:T(8,128)(2,1)}, ...), branch_computations={%region_98.99_spmd, %region_99.100_spmd} | conditional | flops 540803072 | bytes 13124148 | solution.py:204
  759.7 8.3 %conditional.58 = (f32[256,4,128]{2,0,1:T(8,128)S(1)}, f32[256,4,128]{2,0,1:T(8,128)S(1)}, bf16[256,4,128]{0,2,1:T(8,128)(2,1)S(1)}) conditional(s32[]{:T(128)} %convert_element_type.252, (f32[256,4,128]{2,0,1:T(8,128)S(1)}, f32[256,4,128]{2,0,1:T(8,128)S(1)}) %get-tuple-element.2423, (pred[512]{0:T(512)(128)(4,1)S(1)}, ...), branch_computations={%region_100.101_spmd, %region_101.102_spmd} | conditional | flops 540803072 | bytes 13910580 | solution.py:204
  769.2 9.1 %conditional.59 = (f32[256,4,128]{2,0,1:T(8,128)S(1)}, bf16[1,256,512]{2,1,0:T(8,128)(2,1)S(1)}) conditional(s32[]{:T(128)} %convert_element_type.251, (f32[256,4,128]{2,0,1:T(8,128)S(1)}, bf16[256,4,128]{0,2,1:T(8,128)(2,1)S(1)}) %tuple.411, (pred[512]{0:T(512)(128)(4,1)S(1)}, bf16[512,4,128]{0,2,1:T(8,128)(2,1)}, ...), branch_computations={%region_102.103_spmd, %region_103.104_spmd} | conditional | flops 540934144 | bytes 12337680 | solution.py:204
  (644 shorter events, 648.5 us)
Async XLA Ops:
  7.2 681.4 %all-reduce.12.cloned.1.call-start = ((), (), s32[]{:S(2)}) async-start(), calls=%async_computation | async-start | bytes 4194304 | tf_op jit(solution)/shard_map/psum | solution.py:244
  8.4 51.2 %collective-permute-start = (bf16[256,4,128]{0,2,1:T(8,128)(2,1)S(1)}, bf16[256,4,128]{0,2,1:T(8,128)(2,1)}, u32[]{:S(2)}, u32[]{:S(2)}) collective-permute-start(bf16[256,4,128]{0,2,1:T(8,128)(2,1)S(1)} %bitcast.441), channel_id=1, source_target_pairs={{0,8},{8,16},{16,24},{24,32},{32,40},{40,48},{48,56},{56,64},{64,7... | collective-permute-start | bytes 786440 | tf_op jit(solution)/shard_map/ppermute | solution.py:16
  10.3 61.1 %collective-permute-start.20 = (bf16[256,4,128]{0,2,1:T(8,128)(2,1)S(1)}, bf16[256,4,128]{0,2,1:T(8,128)(2,1)}, u32[]{:S(2)}, u32[]{:S(2)}) collective-permute-start(bf16[256,4,128]{0,2,1:T(8,128)(2,1)S(1)} %bitcast.442), channel_id=1, source_target_pairs={{8,0},{16,8},{24,16},{32,24},{40,32},{48,40},{56,48},{64,56},{72,6... | collective-permute-start | bytes 786440 | tf_op jit(solution)/shard_map/ppermute | solution.py:16
  18.7 48.1 %collective-permute-start.2 = (bf16[256,4,128]{0,2,1:T(8,128)(2,1)S(1)}, bf16[256,4,128]{0,2,1:T(8,128)(2,1)}, u32[]{:S(2)}, u32[]{:S(2)}) collective-permute-start(bf16[256,4,128]{0,2,1:T(8,128)(2,1)S(1)} %bitcast.414), channel_id=1, source_target_pairs={{0,8},{8,16},{16,24},{24,32},{32,40},{40,48},{48,56},{56,64},{64,7... | collective-permute-start | bytes 786440 | tf_op jit(solution)/shard_map/ppermute | solution.py:16
  20.6 56.4 %collective-permute-start.22 = (bf16[256,4,128]{0,2,1:T(8,128)(2,1)S(1)}, bf16[256,4,128]{0,2,1:T(8,128)(2,1)}, u32[]{:S(2)}, u32[]{:S(2)}) collective-permute-start(bf16[256,4,128]{0,2,1:T(8,128)(2,1)S(1)} %bitcast.415), channel_id=1, source_target_pairs={{8,0},{16,8},{24,16},{32,24},{40,32},{48,40},{56,48},{64,56},{72,6... | collective-permute-start | bytes 786440 | tf_op jit(solution)/shard_map/ppermute | solution.py:16
  29.0 44.4 %collective-permute-start.40 = (bf16[256,4,128]{0,2,1:T(8,128)(2,1)S(1)}, bf16[256,4,128]{0,2,1:T(8,128)(2,1)}, u32[]{:S(2)}, u32[]{:S(2)}) collective-permute-start(bf16[256,4,128]{0,2,1:T(8,128)(2,1)S(1)} %bitcast.390), channel_id=1, source_target_pairs={{0,8},{8,16},{16,24},{24,32},{32,40},{40,48},{48,56},{56,64},{64,7... | collective-permute-start | bytes 786440 | tf_op jit(solution)/shard_map/ppermute | solution.py:16
  200.9 35.4 %collective-permute-start.64 = (bf16[256,4,128]{0,2,1:T(8,128)(2,1)}, bf16[256,4,128]{0,2,1:T(8,128)(2,1)}, u32[]{:S(2)}, u32[]{:S(2)}) collective-permute-start(bf16[256,4,128]{0,2,1:T(8,128)(2,1)} %collective-permute-done.57), channel_id=1, source_target_pairs={{0,8},{8,16},{16,24},{24,32},{32,40},{40,48},{48,56},{56,64},{64,7... | collective-permute-start | bytes 786440 | tf_op jit(solution)/shard_map/ppermute | solution.py:16
  290.4 36.4 %collective-permute-start.37 = (bf16[256,4,128]{0,2,1:T(8,128)(2,1)S(1)}, bf16[256,4,128]{0,2,1:T(8,128)(2,1)}, u32[]{:S(2)}, u32[]{:S(2)}) collective-permute-start(bf16[256,4,128]{0,2,1:T(8,128)(2,1)S(1)} %collective-permute-done.36), channel_id=1, source_target_pairs={{8,0},{16,8},{24,16},{32,24},{40,32},{48,40},{56,48},{64,56},{72,6... | collective-permute-start | bytes 786440 | tf_op jit(solution)/shard_map/ppermute | solution.py:16
  301.8 102.2 %collective-permute-start.73 = (bf16[256,4,128]{0,2,1:T(8,128)(2,1)}, bf16[256,4,128]{0,2,1:T(8,128)(2,1)}, u32[]{:S(2)}, u32[]{:S(2)}) collective-permute-start(bf16[256,4,128]{0,2,1:T(8,128)(2,1)} %collective-permute-done.72), channel_id=1, source_target_pairs={{0,8},{8,16},{16,24},{24,32},{32,40},{40,48},{48,56},{56,64},{64,7... | collective-permute-start | bytes 786440 | tf_op jit(solution)/shard_map/ppermute | solution.py:16
  303.7 95.4 %collective-permute-start.113 = (bf16[256,4,128]{0,2,1:T(8,128)(2,1)}, bf16[256,4,128]{0,2,1:T(8,128)(2,1)}, u32[]{:S(2)}, u32[]{:S(2)}) collective-permute-start(bf16[256,4,128]{0,2,1:T(8,128)(2,1)} %collective-permute-done.112), channel_id=1, source_target_pairs={{8,0},{16,8},{24,16},{32,24},{40,32},{48,40},{56,48},{64,56},{72,6... | collective-permute-start | bytes 786440 | tf_op jit(solution)/shard_map/ppermute | solution.py:16
  344.0 72.2 %collective-permute-start.42 = (f32[4,256]{1,0:T(4,128)S(1)}, f32[4,256]{1,0:T(4,128)}, u32[]{:S(2)}, u32[]{:S(2)}) collective-permute-start(f32[4,256]{1,0:T(4,128)S(1)} %log_add_fusion), channel_id=1, source_target_pairs={{0,8},{8,16},{16,24},{24,32},{32,40},{40,48},{48,56},{56,64},{64,7... | collective-permute-start | bytes 12296 | tf_op jit(solution)/shard_map/ppermute | solution.py:16
  345.9 60.0 %collective-permute-start.46 = (f32[4,256]{0,1:T(8,128)S(1)}, f32[4,256]{0,1:T(8,128)}, u32[]{:S(2)}, u32[]{:S(2)}) collective-permute-start(f32[4,256]{0,1:T(8,128)S(1)} %bitcast.429), channel_id=1, source_target_pairs={{0,8},{8,16},{16,24},{24,32},{32,40},{40,48},{48,56},{56,64},{64,7... | collective-permute-start | bytes 12296 | tf_op jit(solution)/shard_map/ppermute | solution.py:16
  347.8 73.8 %collective-permute-start.82 = (f32[4,256]{1,0:T(4,128)S(1)}, f32[4,256]{1,0:T(4,128)S(1)}, u32[]{:S(2)}, u32[]{:S(2)}) collective-permute-start(f32[4,256]{1,0:T(4,128)S(1)} %log_add_fusion), channel_id=1, source_target_pairs={{8,0},{16,8},{24,16},{32,24},{40,32},{48,40},{56,48},{64,56},{72,6... | collective-permute-start | bytes 12296 | tf_op jit(solution)/shard_map/ppermute | solution.py:16
  399.1 74.6 %collective-permute-start.84 = (bf16[256,4,128]{0,2,1:T(8,128)(2,1)}, bf16[256,4,128]{0,2,1:T(8,128)(2,1)S(1)}, u32[]{:S(2)}, u32[]{:S(2)}) collective-permute-start(bf16[256,4,128]{0,2,1:T(8,128)(2,1)} %copy.612), channel_id=1, source_target_pairs={{8,0},{16,8},{24,16},{32,24},{40,32},{48,40},{56,48},{64,56},{72,6... | collective-permute-start | bytes 786440 | tf_op jit(solution)/shard_map/ppermute | solution.py:16
  412.4 59.5 %collective-permute-start.44 = (bf16[256,4,128]{2,0,1:T(8,128)(2,1)S(1)}, bf16[256,4,128]{2,0,1:T(8,128)(2,1)S(1)}, u32[]{:S(2)}, u32[]{:S(2)}) collective-permute-start(bf16[256,4,128]{2,0,1:T(8,128)(2,1)S(1)} %copy_bitcast_fusion), channel_id=1, source_target_pairs={{0,8},{8,16},{16,24},{24,32},{32,40},{40,48},{48,56},{56,64},{64,7... | collective-permute-start | bytes 786440 | tf_op jit(solution)/shard_map/ppermute | solution.py:16
  471.8 39.7 %collective-permute-start.45 = (bf16[256,4,128]{2,0,1:T(8,128)(2,1)S(1)}, bf16[256,4,128]{2,0,1:T(8,128)(2,1)S(1)}, u32[]{:S(2)}, u32[]{:S(2)}) collective-permute-start(bf16[256,4,128]{2,0,1:T(8,128)(2,1)S(1)} %collective-permute-done.44), channel_id=1, source_target_pairs={{0,8},{8,16},{16,24},{24,32},{32,40},{40,48},{48,56},{56,64},{64,7... | collective-permute-start | bytes 786440 | tf_op jit(solution)/shard_map/ppermute | solution.py:16
  473.8 39.7 %collective-permute-start.85 = (bf16[256,4,128]{0,2,1:T(8,128)(2,1)S(1)}, bf16[256,4,128]{0,2,1:T(8,128)(2,1)S(1)}, u32[]{:S(2)}, u32[]{:S(2)}) collective-permute-start(bf16[256,4,128]{0,2,1:T(8,128)(2,1)S(1)} %collective-permute-done.84), channel_id=1, source_target_pairs={{8,0},{16,8},{24,16},{32,24},{40,32},{48,40},{56,48},{64,56},{72,6... | collective-permute-start | bytes 786440 | tf_op jit(solution)/shard_map/ppermute | solution.py:16
  511.5 36.9 %collective-permute-start.52 = (bf16[256,4,128]{2,0,1:T(8,128)(2,1)S(1)}, bf16[256,4,128]{2,0,1:T(8,128)(2,1)}, u32[]{:S(2)}, u32[]{:S(2)}) collective-permute-start(bf16[256,4,128]{2,0,1:T(8,128)(2,1)S(1)} %collective-permute-done.45), channel_id=1, source_target_pairs={{0,8},{8,16},{16,24},{24,32},{32,40},{40,48},{48,56},{56,64},{64,7... | collective-permute-start | bytes 786440 | tf_op jit(solution)/shard_map/ppermute | solution.py:16
  513.5 36.9 %collective-permute-start.92 = (bf16[256,4,128]{0,2,1:T(8,128)(2,1)S(1)}, bf16[256,4,128]{0,2,1:T(8,128)(2,1)S(1)}, u32[]{:S(2)}, u32[]{:S(2)}) collective-permute-start(bf16[256,4,128]{0,2,1:T(8,128)(2,1)S(1)} %collective-permute-done.85), channel_id=1, source_target_pairs={{8,0},{16,8},{24,16},{32,24},{40,32},{48,40},{56,48},{64,56},{72,6... | collective-permute-start | bytes 786440 | tf_op jit(solution)/shard_map/ppermute | solution.py:16
  548.4 46.1 %collective-permute-start.53 = (bf16[256,4,128]{2,0,1:T(8,128)(2,1)}, bf16[256,4,128]{2,0,1:T(8,128)(2,1)}, u32[]{:S(2)}, u32[]{:S(2)}) collective-permute-start(bf16[256,4,128]{2,0,1:T(8,128)(2,1)} %collective-permute-done.52), channel_id=1, source_target_pairs={{0,8},{8,16},{16,24},{24,32},{32,40},{40,48},{48,56},{56,64},{64,7... | collective-permute-start | bytes 786440 | tf_op jit(solution)/shard_map/ppermute | solution.py:16
  550.4 46.1 %collective-permute-start.93 = (bf16[256,4,128]{0,2,1:T(8,128)(2,1)S(1)}, bf16[256,4,128]{0,2,1:T(8,128)(2,1)}, u32[]{:S(2)}, u32[]{:S(2)}) collective-permute-start(bf16[256,4,128]{0,2,1:T(8,128)(2,1)S(1)} %collective-permute-done.92), channel_id=1, source_target_pairs={{8,0},{16,8},{24,16},{32,24},{40,32},{48,40},{56,48},{64,56},{72,6... | collective-permute-start | bytes 786440 | tf_op jit(solution)/shard_map/ppermute | solution.py:16
  594.5 54.6 %collective-permute-start.60 = (bf16[256,4,128]{2,0,1:T(8,128)(2,1)}, bf16[256,4,128]{2,0,1:T(8,128)(2,1)}, u32[]{:S(2)}, u32[]{:S(2)}) collective-permute-start(bf16[256,4,128]{2,0,1:T(8,128)(2,1)} %collective-permute-done.53), channel_id=1, source_target_pairs={{0,8},{8,16},{16,24},{24,32},{32,40},{40,48},{48,56},{56,64},{64,7... | collective-permute-start | bytes 786440 | tf_op jit(solution)/shard_map/ppermute | solution.py:16
  596.5 54.6 %collective-permute-start.100 = (bf16[256,4,128]{0,2,1:T(8,128)(2,1)}, bf16[256,4,128]{0,2,1:T(8,128)(2,1)}, u32[]{:S(2)}, u32[]{:S(2)}) collective-permute-start(bf16[256,4,128]{0,2,1:T(8,128)(2,1)} %collective-permute-done.93), channel_id=1, source_target_pairs={{8,0},{16,8},{24,16},{32,24},{40,32},{48,40},{56,48},{64,56},{72,6... | collective-permute-start | bytes 786440 | tf_op jit(solution)/shard_map/ppermute | solution.py:16
  710.2 57.9 %collective-permute-start.117 = (bf16[256,4,128]{0,2,1:T(8,128)(2,1)}, bf16[256,4,128]{0,2,1:T(8,128)(2,1)}, u32[]{:S(2)}, u32[]{:S(2)}) collective-permute-start(bf16[256,4,128]{0,2,1:T(8,128)(2,1)} %collective-permute-done.116), channel_id=1, source_target_pairs={{8,0},{16,8},{24,16},{32,24},{40,32},{48,40},{56,48},{64,56},{72,6... | collective-permute-start | bytes 786440 | tf_op jit(solution)/shard_map/ppermute | solution.py:16
  (187 other events, 5690.3 us)
Sparse Core Ops, SparseCore 0:
  404.1 259.7 all-reduce.11
where the time goes:
time: 802 us; the launch traced here: 787 us
  starting transfers between devices  484 us (60%)
  matrix products  95.1 us (12%)
  local copies, waits for them, and re-layouts  89.4 us (11%)
  other arithmetic  67.9 us (8%)
  between operations  42.8 us (5%)
    ppermute x120, starting transfers between devices, from_behind(): return lax.ppermute(value, axis, pairs)  484 us
    concatenate x40, other arithmetic, join_group(): jnp.concatenate([element[0][member_id] for element in waiting], axis=join...  56.2 us
    dot_general x16, matrix products, block_scores(): jnp.einsum('qhe,khe->hqk', queries, key_heads, preferred_element_type=jnp...  37.8 us
    unnamed x167, local copies, waits for them, and re-layouts  34.6 us
    concatenate x20, local copies, waits for them, and re-layouts, join_group(): jnp.concatenate([element[0][member_id] for element in waiting], axis=join...  22.6 us
    dot_general x6, matrix products, query_term(): jnp.einsum('hqk,khe->qhe', grad_scores, key_heads, preferred_element_type...  20.3 us
    ppermute x20, local copies, waits for them, and re-layouts, from_behind(): return lax.ppermute(value, axis, pairs)  18.3 us
  transfers between devices with their start and end apart: 121, of which 1 were waited for; matrix products, arithmetic and copies ran while one was open for 29% of the time, Pallas kernels for 0%

commit v1 on v0

v1 whole, which is shorter than its diff:
```python
import functools
import math

import jax
import jax.numpy as jnp
from jax import lax
from jax.experimental import pallas as pl
from jax.experimental.pallas import tpu as pltpu
from jax.sharding import PartitionSpec as P

HEADS = 4
HEAD = 128
MOST = 11
TOK = 256
D = 1024
ATT = 512
WINDOW = 26
CROSS = 5
FACTOR = 1.0 / math.sqrt(HEAD)
SCALE2 = FACTOR * math.log2(math.e)
FAR = 1e30
MESH = pl.DeviceIdType.MESH
F32 = jnp.float32
BF16 = jnp.bfloat16


def dot(a, b, dims):
    return lax.dot_general(a, b, (dims, ((), ())), preferred_element_type=F32)


NT = ((1,), (1,))
NN = ((1,), (0,))
TN = ((0,), (0,))


def kernel(
    start_ref, count_ref, q_ref, k_ref, v_ref, cot_ref, w_ref,
    proj_ref, gq_ref, gk_ref, gv_ref, gw_ref,
    kv, qd, pack_kv, pack_q, pack_d, stats, lse_col, dot_col, scores,
    out_send, out_home, grad_send, grad_home,
    wp, wc, rc, wx, rx, wy, ry, rz, fz, gwf,
    s1_s, s1_r, s2_s, s2_r, c1_s, c1_r, c2_s, c2_r, s3_s, s3_r, cx_s, cx_r,
    st_s, st_r, o_s, o_r, g_s, g_r, ar_s, ar_r, az_s, az_r,
):
    ctx = lax.axis_index("ctx")
    dp = lax.axis_index("dp")
    yh, z, core = ctx // 16, (ctx // 2) % 8, ctx % 2
    yl, x = dp // 4, dp % 4
    y = yh * 2 + yl
    side = 2 * (z % 2) - 1
    head = z // 2
    partner = (z - side + 8) % 8

    def at(yh_=None, z_=None, core_=None):
        a = yh if yh_ is None else yh_
        b = z if z_ is None else z_
        c = core if core_ is None else core_
        return (a * 16 + b * 2 + c, dp)

    def at_x(o):
        return (ctx, yl * 4 + (x + o) % 4)

    def at_y(o):
        y2 = (y + o) % 4
        return ((y2 // 2) * 16 + z * 2 + core, (y2 % 2) * 4 + x)

    other_core = at(core_=1 - core)
    other_row = at(yh_=1 - yh)
    near = at(z_=partner)

    def own_z(k):
        return (z + side * k + 8) % 8

    def their_z(k):
        return (z - side * (k + 1) + 8) % 8

    def slot(zz, cc):
        return 10 * yh + 2 * zz + cc

    targets = [None, (z + side + 8) % 8, (z - 2 * side + 8) % 8, (z + 3 * side + 8) % 8]

    def remote(src, dst, ss, rs, device):
        return pltpu.make_async_remote_copy(
            src_ref=src, dst_ref=dst, send_sem=ss, recv_sem=rs, device_id=device, device_id_type=MESH
        )

    peers = [other_core, at(z_=partner, core_=1 - core)]
    peers += [at(z_=(z + o) % 8) for o in range(1, 8)]
    peers += [at_x(o) for o in range(1, 4)]
    peers += [at_y(o) for o in range(1, 4)]
    peers += [
        at(1 - yh, z, 1 - core),
        at(1 - yh, partner, core),
        at(1 - yh, partner, 1 - core),
    ]
    barrier = pltpu.get_barrier_semaphore()
    for peer in peers:
        pl.semaphore_signal(barrier, inc=1, device_id=peer, device_id_type=MESH)
    for h in range(HEADS):
        cols = slice(h * HEAD, (h + 1) * HEAD)
        pack_kv[h, 0] = k_ref[:, cols]
        pack_kv[h, 1] = v_ref[:, cols]
        pack_q[h] = q_ref[:, cols]
    pl.semaphore_wait(barrier, len(peers))

    home = slot(z, core)

    def leg1(kind, k):
        t = targets[k]
        if kind == 0:
            src, dst = pack_kv.at[t // 2], kv.at[home]
        elif kind == 1:
            src, dst = pack_q.at[t // 2], qd.at[home, 0]
        else:
            src, dst = pack_d.at[t // 2], qd.at[home, 1]
        return remote(src, dst, s1_s.at[kind, k], s1_r.at[kind, k], at(z_=t))

    for kind in (0, 1):
        for k in (1, 2, 3):
            leg1(kind, k).start()
    kv[home] = pack_kv[head]
    qd[home, 0] = pack_q[head]

    bufs = (kv, qd)

    def leg2(g, k):
        sl = slot(own_z(k), core)
        return remote(bufs[g].at[sl], bufs[g].at[sl], s2_s.at[g, k], s2_r.at[g, k], near)

    def core1(g, k):
        sl = slot(own_z(k), core)
        return remote(bufs[g].at[sl], bufs[g].at[sl], c1_s.at[g, k], c1_r.at[g, k], other_core)

    def core2(g, k):
        sl = slot(their_z(k), core)
        return remote(bufs[g].at[sl], bufs[g].at[sl], c2_s.at[g, k], c2_r.at[g, k], other_core)

    def leg3(g, m):
        src = slot(m + 3 * (1 - yh), core)
        dst = 2 * m + core + 16 * yh
        return remote(bufs[g].at[src], bufs[g].at[dst], s3_s.at[g, m], s3_r.at[g, m], other_row)

    def cross_core(g, m):
        sl = 2 * m + core + 16 * (1 - yh)
        return remote(bufs[g].at[sl], bufs[g].at[sl], cx_s.at[g, m], cx_r.at[g, m], other_core)

    def maybe_leg3(g, zz):
        m = zz - 3 * (1 - yh)

        @pl.when(jnp.logical_and(m >= 0, m < CROSS))
        def _():
            leg3(g, m).start()

    def spread_own(g, k):
        leg2(g, k).start()
        maybe_leg3(g, own_z(k))
        core1(g, k).start()

    def spread_their(g, k):
        leg2(g, k).wait_recv()
        maybe_leg3(g, their_z(k))
        core2(g, k).start()

    def spread_cross(g, m):
        leg3(g, m).wait_recv()
        cross_core(g, m).start()

    def all_here(g):
        for k in range(4):
            core1(g, k).wait_recv()
            core2(g, k).wait_recv()
        for m in range(CROSS):
            cross_core(g, m).wait_recv()

    spread_own(0, 0)
    grad_att = dot(cot_ref[...], w_ref[...], NT).astype(BF16)
    for h in range(HEADS):
        pack_d[h] = grad_att[:, h * HEAD : (h + 1) * HEAD]
    qd[home, 1] = pack_d[head]
    for k in (1, 2, 3):
        leg1(0, k).wait_recv()
        spread_own(0, k)
    for k in (1, 2, 3):
        leg1(2, k).start()
    for k in range(4):
        spread_their(0, k)
    for m in range(CROSS):
        spread_cross(0, m)
    for k in (1, 2, 3):
        leg1(1, k).wait_recv()
        leg1(2, k).wait_recv()
    all_here(0)

    member = yh * 4 + (z % 2) * 2 + core

    def send_out(k):
        return remote(out_send.at[k], out_home.at[head], o_s.at[k], o_r.at[k], at(z_=own_z(k)))

    def block_range(k):
        block = 16 * yh + 2 * own_z(k) + core
        return start_ref[block] - 6 * yh, count_ref[block]

    def nth(first, count, t):
        return jnp.clip(first + jnp.minimum(t, count - 1), 0, WINDOW - 1)

    def pen(t, count):
        return jnp.where(t < count, 0.0, FAR)

    def forward_block(k, carry):
        @pl.when(k == 0)
        def _():
            for j in range(4):
                spread_own(1, j)

        sl = slot(own_z(k), core)
        first, count = block_range(k)
        query = qd[sl, 0]
        top = None
        for t in range(MOST):
            other = nth(first, count, t)
            s = dot(query, kv[other, 0], NT)
            scores[t] = s
            top = s if top is None else jnp.maximum(top, s)
        peak = jnp.max(top, axis=1, keepdims=True) * SCALE2
        total = jnp.zeros((TOK, HEAD), F32)
        acc = jnp.zeros((TOK, HEAD), F32)
        for t in range(MOST):
            other = nth(first, count, t)
            p = jnp.exp2(scores[t] * SCALE2 - (peak + pen(t, count)))
            total = total + (p[:, :HEAD] + p[:, HEAD:])
            acc = acc + dot(p.astype(BF16), kv[other, 1], NN)
        sums = jnp.sum(total, axis=1, keepdims=True)
        attended = (acc / sums).astype(BF16)
        out_send[k] = attended
        lse = peak + jnp.log2(sums)
        rd = jnp.sum(qd[sl, 1].astype(F32) * attended.astype(F32), axis=1, keepdims=True)
        lse_col[k] = jnp.broadcast_to(lse, (TOK, HEAD))
        dot_col[k] = jnp.broadcast_to(rd, (TOK, HEAD))
        lane = lax.broadcasted_iota(jnp.int32, (TOK, HEAD), 1)
        turned = jnp.where(lane < 8, lse, rd).T
        stats[member, k] = turned[:16]

        @pl.when(k == 0)
        def _():
            out_home[head] = out_send[0]

        @pl.when(k > 0)
        def _():
            send_out(k).start()

        @pl.when(k == 1)
        def _():
            for j in range(4):
                spread_their(1, j)

        @pl.when(k == 3)
        def _():
            for m in range(CROSS):
                spread_cross(1, m)

        return carry

    lax.fori_loop(0, 4, forward_block, 0)

    quad = [
        other_core, near, at(z_=partner, core_=1 - core), other_row,
        at(1 - yh, z, 1 - core), at(1 - yh, partner, core), at(1 - yh, partner, 1 - core),
    ]

    def send_stats(i):
        return remote(stats.at[member], stats.at[member], st_s.at[i], st_r.at[i], quad[i])

    for i in range(7):
        send_stats(i).start()

    def home_out(k):
        t = targets[k]
        return remote(out_send.at[k], out_home.at[t // 2], o_s.at[k], o_r.at[k], at(z_=t))

    def ar_core():
        return remote(wp.at[1 - core], rc, ar_s.at[0], ar_r.at[0], other_core)

    def ar_x(o):
        return remote(wc.at[(x + o) % 4], rx.at[o - 1], ar_s.at[o], ar_r.at[o], at_x(o))

    def ar_y(o):
        return remote(wx.at[(y + o) % 4], ry.at[o - 1], ar_s.at[3 + o], ar_r.at[3 + o], at_y(o))

    def ar_z(o):
        t = (z + o) % 8
        return remote(wy.at[t], rz.at[o - 1], az_s.at[0, o], az_r.at[0, o], at(z_=t))

    def back_z(o):
        return remote(fz.at[z], fz.at[z], az_s.at[1, o], az_r.at[1, o], at(z_=(z + o) % 8))

    def back_y(o):
        part = gwf.at[core, x, y]
        return remote(part, part, ar_s.at[6 + o], ar_r.at[6 + o], at_y(o))

    def back_x(o):
        part = gwf.at[core, x]
        return remote(part, part, ar_s.at[9 + o], ar_r.at[9 + o], at_x(o))

    def back_core():
        return remote(gwf.at[core], gwf.at[core], ar_s.at[13], ar_r.at[13], other_core)

    def weight_term():
        for k in (1, 2, 3):
            home_out(k).wait_recv()
        for h in range(HEADS):
            part = dot(out_home[h], cot_ref[...], TN).astype(BF16)
            for piece in range(8):
                row = h * 8 + piece
                wp[row // 16, (row // 4) % 4, row % 4] = part[piece * 16 : (piece + 1) * 16]
        ar_core().start()

    def sum_core():
        ar_core().wait_recv()
        wc[...] = (wp[core].astype(F32) + rc[...].astype(F32)).astype(BF16)
        for o in (1, 2, 3):
            ar_x(o).start()

    def sum_x():
        total = wc[x].astype(F32)
        for o in (1, 2, 3):
            ar_x(o).wait_recv()
            total = total + rx[o - 1].astype(F32)
        wx[...] = total.astype(BF16)
        for o in (1, 2, 3):
            ar_y(o).start()

    def sum_y():
        total = wx[y].astype(F32)
        for o in (1, 2, 3):
            ar_y(o).wait_recv()
            total = total + ry[o - 1].astype(F32)
        total = total.astype(BF16)
        for j in range(8):
            wy[j] = total[:, j * HEAD : (j + 1) * HEAD]
        for o in range(1, 8):
            ar_z(o).start()

    def sum_z():
        total = wy[z].astype(F32)
        for o in range(1, 8):
            ar_z(o).wait_recv()
            total = total + rz[o - 1].astype(F32)
        rows = TOK * lax.axis_size("ctx") * lax.axis_size("dp")
        fz[z] = (total * (1.0 / math.sqrt(rows))).astype(BF16)
        for o in range(1, 8):
            back_z(o).start()

    def gather_z():
        for o in range(1, 8):
            back_z(o).wait_recv()
        for j in range(8):
            gwf[core, x, y, :, j * HEAD : (j + 1) * HEAD] = fz[j]
        for o in (1, 2, 3):
            back_y(o).start()

    def gather_y():
        for o in (1, 2, 3):
            back_y(o).wait_recv()
        for o in (1, 2, 3):
            back_x(o).start()

    def gather_x():
        for o in (1, 2, 3):
            back_x(o).wait_recv()
        back_core().start()

    def send_grad(a, k):
        return remote(
            grad_send.at[a, k], grad_home.at[a, head], g_s.at[a, k], g_r.at[a, k], at(z_=own_z(k))
        )

    def give_grad(a, k, value):
        grad_send[a, k] = value

        @pl.when(k == 0)
        def _():
            grad_home[a, head] = grad_send[a, 0]

        @pl.when(k > 0)
        def _():
            send_grad(a, k).start()

    def query_block(k, carry):
        @pl.when(k == 2)
        def _():
            weight_term()

        @pl.when(k == 3)
        def _():
            sum_core()

        sl = slot(own_z(k), core)
        first, count = block_range(k)
        query, grad = qd[sl, 0], qd[sl, 1]
        lse = lse_col[k][:, :1]
        rd = dot_col[k][:, :1]
        acc = jnp.zeros((TOK, HEAD), F32)
        for t in range(MOST):
            other = nth(first, count, t)
            keys = kv[other, 0]
            p = jnp.exp2(dot(query, keys, NT) * SCALE2 - (lse + pen(t, count)))
            ds = (p * (dot(grad, kv[other, 1], NT) - rd)).astype(BF16)
            acc = acc + dot(ds, keys, NN)
        give_grad(0, k, (acc * FACTOR).astype(BF16))
        return carry

    lax.fori_loop(0, 4, query_block, 0)

    all_here(1)
    for i in range(7):
        send_stats(i).wait_recv()

    def key_block(k, carry):
        @pl.when(k == 0)
        def _():
            sum_x()

        @pl.when(k == 1)
        def _():
            sum_y()

        @pl.when(k == 2)
        def _():
            sum_z()

        @pl.when(k == 3)
        def _():
            gather_z()

        sl = slot(own_z(k), core)
        first, count = block_range(k)
        keys, values = kv[sl, 0], kv[sl, 1]
        acc_k = jnp.zeros((TOK, HEAD), F32)
        acc_v = jnp.zeros((TOK, HEAD), F32)
        for t in range(MOST):
            other = nth(first, count, t)
            block = other + 6 * yh
            oz = (block // 2) % 8
            left = (2 * head - oz + 8) % 8
            in_left = left < 4
            k_of = jnp.where(in_left, left, 7 - left)
            who = (block // 16) * 4 + jnp.where(in_left, 0, 2) + block % 2
            lse = stats[who, k_of, 0:1, :]
            rd = stats[who, k_of, 8:9, :]
            query, grad = qd[other, 0], qd[other, 1]
            p = jnp.exp2(dot(keys, query, NT) * SCALE2 - (lse + pen(t, count)))
            acc_v = acc_v + dot(p.astype(BF16), grad, NN)
            ds = (p * (dot(values, grad, NT) - rd)).astype(BF16)
            acc_k = acc_k + dot(ds, query, NN)
        give_grad(1, k, (acc_k * FACTOR).astype(BF16))
        give_grad(2, k, acc_v.astype(BF16))
        return carry

    lax.fori_loop(0, 4, key_block, 0)

    gather_y()
    projected = dot(out_home[0], w_ref[0:HEAD], NN)
    for h in range(1, HEADS):
        projected = projected + dot(out_home[h], w_ref[h * HEAD : (h + 1) * HEAD], NN)
    proj_ref[...] = projected.astype(BF16)
    gather_x()

    def home_grad(a, k):
        t = targets[k]
        return remote(
            grad_send.at[a, k], grad_home.at[a, t // 2], g_s.at[a, k], g_r.at[a, k], at(z_=t)
        )

    for a, ref in enumerate((gq_ref, gk_ref, gv_ref)):
        for k in (1, 2, 3):
            home_grad(a, k).wait_recv()
        for h in range(HEADS):
            ref[:, h * HEAD : (h + 1) * HEAD] = grad_home[a, h]
    back_core().wait_recv()
    for a in range(2):
        for b in range(4):
            for c in range(4):
                row = a * 256 + b * 64 + c * 16
                gw_ref[row : row + 16] = gwf[a, b, c]

    for k in (1, 2, 3):
        for kind in range(3):
            leg1(kind, k).wait_send()
        send_out(k).wait_send()
        for a in range(3):
            send_grad(a, k).wait_send()
    for g in range(2):
        for k in range(4):
            leg2(g, k).wait_send()
            core1(g, k).wait_send()
            core2(g, k).wait_send()
        for m in range(CROSS):
            leg3(g, m).wait_send()
            cross_core(g, m).wait_send()
    for i in range(7):
        send_stats(i).wait_send()
    ar_core().wait_send()
    for o in (1, 2, 3):
        for make in (ar_x, ar_y, back_y, back_x):
            make(o).wait_send()
    for o in range(1, 8):
        ar_z(o).wait_send()
        back_z(o).wait_send()
    back_core().wait_send()


def on_device(query_rows, key_rows, value_rows, recordings, out_weight, cotangent):
    labels = recordings[0]
    start = jnp.sum(labels[None, :] < labels[:, None], axis=1).astype(jnp.int32)
    count = jnp.sum(labels[None, :] == labels[:, None], axis=1).astype(jnp.int32)
    vmem = pl.BlockSpec(memory_space=pltpu.VMEM)
    smem = pl.BlockSpec(memory_space=pltpu.SMEM)
    dma = pltpu.SemaphoreType.DMA
    outs = pl.pallas_call(
        kernel,
        out_shape=(
            jax.ShapeDtypeStruct((TOK, D), BF16),
            jax.ShapeDtypeStruct((TOK, ATT), BF16),
            jax.ShapeDtypeStruct((TOK, ATT), BF16),
            jax.ShapeDtypeStruct((TOK, ATT), BF16),
            jax.ShapeDtypeStruct((ATT, D), BF16),
        ),
        in_specs=[smem, smem, vmem, vmem, vmem, vmem, vmem],
        out_specs=(vmem,) * 5,
        scratch_shapes=[
            pltpu.VMEM((WINDOW, 2, TOK, HEAD), BF16),
            pltpu.VMEM((WINDOW, 2, TOK, HEAD), BF16),
            pltpu.VMEM((HEADS, 2, TOK, HEAD), BF16),
            pltpu.VMEM((HEADS, TOK, HEAD), BF16),
            pltpu.VMEM((HEADS, TOK, HEAD), BF16),
            pltpu.VMEM((8, 4, 16, TOK), F32),
            pltpu.VMEM((4, TOK, HEAD), F32),
            pltpu.VMEM((4, TOK, HEAD), F32),
            pltpu.VMEM((MOST, TOK, TOK), F32),
            pltpu.VMEM((4, TOK, HEAD), BF16),
            pltpu.VMEM((HEADS, TOK, HEAD), BF16),
            pltpu.VMEM((3, 4, TOK, HEAD), BF16),
            pltpu.VMEM((3, HEADS, TOK, HEAD), BF16),
            pltpu.VMEM((2, 4, 4, 16, D), BF16),
            pltpu.VMEM((4, 4, 16, D), BF16),
            pltpu.VMEM((4, 4, 16, D), BF16),
            pltpu.VMEM((4, 16, D), BF16),
            pltpu.VMEM((3, 4, 16, D), BF16),
            pltpu.VMEM((8, 16, HEAD), BF16),
            pltpu.VMEM((3, 16, D), BF16),
            pltpu.VMEM((7, 16, HEAD), BF16),
            pltpu.VMEM((8, 16, HEAD), BF16),
            pltpu.VMEM((2, 4, 4, 16, D), BF16),
        ]
        + [dma((3, 4))] * 2
        + [dma((2, 4))] * 6
        + [dma((2, CROSS))] * 4
        + [dma((7,))] * 2
        + [dma((4,))] * 2
        + [dma((3, 4))] * 2
        + [dma((14,))] * 2
        + [dma((2, 8))] * 2,
        compiler_params=pltpu.CompilerParams(
            collective_id=0, has_side_effects=True, vmem_limit_bytes=56 << 20
        ),
    )(start, count, query_rows[0], key_rows[0], value_rows[0], cotangent[0], out_weight)
    projected, grad_query, grad_key, grad_value, grad_weight = outs
    return (projected[None], grad_query[None], grad_key[None], grad_value[None], grad_weight)


def solution(mesh):
    rows = P("dp", "ctx", None)
    return jax.shard_map(
        on_device,
        mesh=mesh,
        in_specs=(rows, rows, rows, P("dp", None), P(), rows),
        out_specs=(rows, rows, rows, rows, P()),
        check_vma=False,
    )
```

time: 802 us -> 117 us (0.15)
  the two profiles are of different devices: /device:TPU:16 before, /device:TPU:1 now
where the time goes in v1:
time: 117 us
  Pallas kernels  110 us (94%)
  local copies, waits for them, and re-layouts  5.68 us (5%)
    pallas_call x1, Pallas kernels, on_device(): pl.pallas_call(kernel, out_shape=(jax.ShapeDtypeStruct((TOK, D), BF16), j...  110 us
    unnamed x15, local copies, waits for them, and re-layouts  5.68 us

profile of v1, /device:TPU:1, one launch (start us, length us, event | category | flops | bytes accessed | tf_op | source)
XLA Modules:
  0.0 116.7 jit_solution(2172216343444355127)
XLA Ops:
  0.6 0.0 copy-start.4
  0.6 0.6 copy-done.4
  1.3 0.7 convert_reduce_fusion
  2.0 109.7 %shard_map.101 = (bf16[256,1024]{1,0:T(8,128)(2,1)}, bf16[256,512]{1,0:T(8,128)(2,1)}, bf16[256,512]{1,0:T(8,128)(2,1)}, bf16[256,512]{1,0:T(8,128)(2,1)}, bf16[512,1024]{1,0:T(8,128)(2,1)}) custom-call(s32[32]{0:T(128)} %get-tuple-element.16.start_ref, s32[32]{0:T(128)} %get-tuple-element.15.count_ref, bf16[256,512]{1,0:T(8,128)(2,1)} %bitcast.11, ...), custom_call_target="tpu_custom_call" | custom-call | tf_op jit(solution)/shard_map/pallas_call | solution.py:519
  111.7 0.0 copy-start.3
  111.7 0.0 copy-start.2
  111.7 0.0 copy-start.1
  111.7 1.9 %copy.16 = bf16[1,256,1024]{2,1,0:T(8,128)(2,1)} copy(bf16[1,256,1024]{2,1,0:T(8,128)(2,1)} %bitcast.9) | data formatting | bytes 1048576
  113.6 0.0 copy-done.3
  113.6 0.0 copy-start
  113.6 0.7 copy.17
  114.3 0.0 copy-done.2
  114.3 0.7 copy.18
  115.1 0.0 copy-done.1
  115.1 0.7 copy.19
  115.8 0.0 copy-done
  115.8 1.0 copy.20
Async XLA Ops:
  0.6 0.7 copy-start.4
  111.7 2.0 %copy-start.3 = (bf16[256,512]{1,0:T(8,128)(2,1)S(1)}, bf16[256,512]{1,0:T(8,128)(2,1)}, u32[]{:S(2)}) copy-start(bf16[256,512]{1,0:T(8,128)(2,1)} %get-tuple-element.11) | copy-start | bytes 786436
  111.7 2.7 %copy-start.2 = (bf16[256,512]{1,0:T(8,128)(2,1)S(1)}, bf16[256,512]{1,0:T(8,128)(2,1)}, u32[]{:S(2)}) copy-start(bf16[256,512]{1,0:T(8,128)(2,1)} %get-tuple-element.12) | copy-start | bytes 786436
  111.7 3.4 %copy-start.1 = (bf16[256,512]{1,0:T(8,128)(2,1)S(1)}, bf16[256,512]{1,0:T(8,128)(2,1)}, u32[]{:S(2)}) copy-start(bf16[256,512]{1,0:T(8,128)(2,1)} %get-tuple-element.13) | copy-start | bytes 786436
  113.6 2.1 %copy-start = (bf16[512,1024]{1,0:T(8,128)(2,1)S(1)}, bf16[512,1024]{1,0:T(8,128)(2,1)}, u32[]{:S(2)}) copy-start(bf16[512,1024]{1,0:T(8,128)(2,1)} %get-tuple-element.26) | copy-start | bytes 3145732

commit v2 on v1

--- a/solution.py
+++ b/solution.py
@@ -14,6 +14,7 @@
 TOK = 256
 D = 1024
 ATT = 512
+BLOCKS = 32
 WINDOW = 26
 CROSS = 5
 FACTOR = 1.0 / math.sqrt(HEAD)
@@ -34,13 +35,14 @@
 
 
 def kernel(
-    start_ref, count_ref, q_ref, k_ref, v_ref, cot_ref, w_ref,
-    proj_ref, gq_ref, gk_ref, gv_ref, gw_ref,
+    rec_ref, q_hbm, k_hbm, v_hbm, cot_hbm, w_hbm,
+    proj_hbm, gq_hbm, gk_hbm, gv_hbm, gw_hbm,
+    cot_ref, w_ref, proj_ref, ranges,
     kv, qd, pack_kv, pack_q, pack_d, stats, lse_col, dot_col, scores,
     out_send, out_home, grad_send, grad_home,
-    wp, wc, rc, wx, rx, wy, ry, rz, fz, gwf,
+    wp, wc, rc, wx, rx, rxy, wz, rz, fz, gwf,
     s1_s, s1_r, s2_s, s2_r, c1_s, c1_r, c2_s, c2_r, s3_s, s3_r, cx_s, cx_r,
-    st_s, st_r, o_s, o_r, g_s, g_r, ar_s, ar_r, az_s, az_r,
+    st_s, st_r, o_s, o_r, g_s, g_r, ar_s, ar_r, az_s, az_r, wb_s, wb_r, in_s, out_s,
 ):
     ctx = lax.axis_index("ctx")
     dp = lax.axis_index("dp")
@@ -83,6 +85,17 @@
         return pltpu.make_async_remote_copy(
             src_ref=src, dst_ref=dst, send_sem=ss, recv_sem=rs, device_id=device, device_id_type=MESH
         )
+
+    loads = []
+    for h in range(HEADS):
+        cols = pl.ds(h * HEAD, HEAD)
+        loads.append((k_hbm.at[:, cols], pack_kv.at[h, 0]))
+        loads.append((v_hbm.at[:, cols], pack_kv.at[h, 1]))
+        loads.append((q_hbm.at[:, cols], pack_q.at[h]))
+    loads += [(cot_hbm, cot_ref), (w_hbm, w_ref)]
+    loads = [pltpu.make_async_copy(src, dst, in_s.at[i]) for i, (src, dst) in enumerate(loads)]
+    for load in loads:
+        load.start()
 
     peers = [other_core, at(z_=partner, core_=1 - core)]
     peers += [at(z_=(z + o) % 8) for o in range(1, 8)]
@@ -96,11 +109,17 @@
     barrier = pltpu.get_barrier_semaphore()
     for peer in peers:
         pl.semaphore_signal(barrier, inc=1, device_id=peer, device_id_type=MESH)
-    for h in range(HEADS):
-        cols = slice(h * HEAD, (h + 1) * HEAD)
-        pack_kv[h, 0] = k_ref[:, cols]
-        pack_kv[h, 1] = v_ref[:, cols]
-        pack_q[h] = q_ref[:, cols]
+    for k in range(4):
+        label = rec_ref[0, 16 * yh + 2 * own_z(k) + core]
+        first = jnp.int32(0)
+        count = jnp.int32(0)
+        for j in range(BLOCKS):
+            first = first + jnp.where(rec_ref[0, j] < label, 1, 0)
+            count = count + jnp.where(rec_ref[0, j] == label, 1, 0)
+        ranges[0, k] = first - 6 * yh
+        ranges[1, k] = count
+    for load in loads[:12]:
+        load.wait()
     pl.semaphore_wait(barrier, len(peers))
 
     home = slot(z, core)
@@ -151,10 +170,13 @@
         def _():
             leg3(g, m).start()
 
+    def spread_row(g, k):
+        leg2(g, k).start()
+        core1(g, k).start()
+
     def spread_own(g, k):
-        leg2(g, k).start()
+        spread_row(g, k)
         maybe_leg3(g, own_z(k))
-        core1(g, k).start()
 
     def spread_their(g, k):
         leg2(g, k).wait_recv()
@@ -173,22 +195,28 @@
             cross_core(g, m).wait_recv()
 
     spread_own(0, 0)
+    for load in loads[12:]:
+        load.wait()
     grad_att = dot(cot_ref[...], w_ref[...], NT).astype(BF16)
     for h in range(HEADS):
         pack_d[h] = grad_att[:, h * HEAD : (h + 1) * HEAD]
     qd[home, 1] = pack_d[head]
     for k in (1, 2, 3):
+        leg1(2, k).start()
+    for k in (1, 2, 3):
         leg1(0, k).wait_recv()
         spread_own(0, k)
-    for k in (1, 2, 3):
-        leg1(2, k).start()
     for k in range(4):
         spread_their(0, k)
-    for m in range(CROSS):
-        spread_cross(0, m)
+    spread_row(1, 0)
     for k in (1, 2, 3):
         leg1(1, k).wait_recv()
         leg1(2, k).wait_recv()
+        spread_row(1, k)
+    for m in range(CROSS):
+        spread_cross(0, m)
+    for k in range(4):
+        maybe_leg3(1, own_z(k))
     all_here(0)
 
     member = yh * 4 + (z % 2) * 2 + core
@@ -197,8 +225,7 @@
         return remote(out_send.at[k], out_home.at[head], o_s.at[k], o_r.at[k], at(z_=own_z(k)))
 
     def block_range(k):
-        block = 16 * yh + 2 * own_z(k) + core
-        return start_ref[block] - 6 * yh, count_ref[block]
+        return ranges[0, k], ranges[1, k]
 
     def nth(first, count, t):
         return jnp.clip(first + jnp.minimum(t, count - 1), 0, WINDOW - 1)
@@ -207,11 +234,6 @@
         return jnp.where(t < count, 0.0, FAR)
 
     def forward_block(k, carry):
-        @pl.when(k == 0)
-        def _():
-            for j in range(4):
-                spread_own(1, j)
-
         sl = slot(own_z(k), core)
         first, count = block_range(k)
         query = qd[sl, 0]
@@ -248,16 +270,6 @@
         def _():
             send_out(k).start()
 
-        @pl.when(k == 1)
-        def _():
-            for j in range(4):
-                spread_their(1, j)
-
-        @pl.when(k == 3)
-        def _():
-            for m in range(CROSS):
-                spread_cross(1, m)
-
         return carry
 
     lax.fori_loop(0, 4, forward_block, 0)
@@ -278,70 +290,94 @@
         return remote(out_send.at[k], out_home.at[t // 2], o_s.at[k], o_r.at[k], at(z_=t))
 
     def ar_core():
-        return remote(wp.at[1 - core], rc, ar_s.at[0], ar_r.at[0], other_core)
-
-    def ar_x(o):
-        return remote(wc.at[(x + o) % 4], rx.at[o - 1], ar_s.at[o], ar_r.at[o], at_x(o))
-
-    def ar_y(o):
-        return remote(wx.at[(y + o) % 4], ry.at[o - 1], ar_s.at[3 + o], ar_r.at[3 + o], at_y(o))
+        return remote(wp.at[1 - core], rc, ar_s.at[4, 0, 0], ar_r.at[4, 0, 0], other_core)
+
+    def step1(half, o):
+        there = at_x(o) if half == 0 else at_y(o)
+        mine = x if half == 0 else y
+        return remote(
+            wc.at[half, (mine + o) % 4], rx.at[half, o - 1], ar_s.at[0, half, o], ar_r.at[0, half, o], there
+        )
+
+    def step2(half, o):
+        there = at_y(o) if half == 0 else at_x(o)
+        mine = y if half == 0 else x
+        return remote(
+            wx.at[half, (mine + o) % 4], rxy.at[half, o - 1], ar_s.at[1, half, o], ar_r.at[1, half, o], there
+        )
 
     def ar_z(o):
         t = (z + o) % 8
-        return remote(wy.at[t], rz.at[o - 1], az_s.at[0, o], az_r.at[0, o], at(z_=t))
+        return remote(wz.at[t], rz.at[o - 1], az_s.at[0, o], az_r.at[0, o], at(z_=t))
 
     def back_z(o):
         return remote(fz.at[z], fz.at[z], az_s.at[1, o], az_r.at[1, o], at(z_=(z + o) % 8))
 
-    def back_y(o):
-        part = gwf.at[core, x, y]
-        return remote(part, part, ar_s.at[6 + o], ar_r.at[6 + o], at_y(o))
-
-    def back_x(o):
-        part = gwf.at[core, x]
-        return remote(part, part, ar_s.at[9 + o], ar_r.at[9 + o], at_x(o))
-
-    def back_core():
-        return remote(gwf.at[core], gwf.at[core], ar_s.at[13], ar_r.at[13], other_core)
+    firsts, seconds = (x, y), (y, x)
+
+    def final_row(half):
+        return pl.multiple_of(firsts[half] * 64 + seconds[half] * 16, 16)
+
+    def back2(half, o):
+        part = gwf.at[core, half, pl.ds(final_row(half), 16)]
+        there = at_y(o) if half == 0 else at_x(o)
+        return remote(part, part, ar_s.at[2, half, o], ar_r.at[2, half, o], there)
+
+    def back1(half, o):
+        part = gwf.at[core, half, pl.ds(pl.multiple_of(firsts[half] * 64, 64), 64)]
+        there = at_x(o) if half == 0 else at_y(o)
+        return remote(part, part, ar_s.at[3, half, o], ar_r.at[3, half, o], there)
+
+    def back_core(half, o):
+        piece = (firsts[half] - o + 4) % 4
+        part = gwf.at[core, half, pl.ds(pl.multiple_of(piece * 64, 64), 64)]
+        return remote(part, part, wb_s.at[half, o], wb_r.at[half, o], other_core)
 
     def weight_term():
         for k in (1, 2, 3):
             home_out(k).wait_recv()
-        for h in range(HEADS):
-            part = dot(out_home[h], cot_ref[...], TN).astype(BF16)
-            for piece in range(8):
-                row = h * 8 + piece
-                wp[row // 16, (row // 4) % 4, row % 4] = part[piece * 16 : (piece + 1) * 16]
-        ar_core().start()
+        for c in (1 - core, core):
+            for i in range(2):
+                part = dot(out_home[2 * c + i], cot_ref[...], TN).astype(BF16)
+                for half in range(2):
+                    for a in range(2):
+                        for b in range(4):
+                            rows = slice(a * 64 + b * 16, a * 64 + b * 16 + 16)
+                            wp[c, half, i * 2 + a, b] = part[rows, half * 512 : half * 512 + 512]
+            if c is not core:
+                ar_core().start()
 
     def sum_core():
         ar_core().wait_recv()
         wc[...] = (wp[core].astype(F32) + rc[...].astype(F32)).astype(BF16)
         for o in (1, 2, 3):
-            ar_x(o).start()
-
-    def sum_x():
-        total = wc[x].astype(F32)
-        for o in (1, 2, 3):
-            ar_x(o).wait_recv()
-            total = total + rx[o - 1].astype(F32)
-        wx[...] = total.astype(BF16)
-        for o in (1, 2, 3):
-            ar_y(o).start()
-
-    def sum_y():
-        total = wx[y].astype(F32)
-        for o in (1, 2, 3):
-            ar_y(o).wait_recv()
-            total = total + ry[o - 1].astype(F32)
-        total = total.astype(BF16)
-        for j in range(8):
-            wy[j] = total[:, j * HEAD : (j + 1) * HEAD]
+            for half in range(2):
+                step1(half, o).start()
+
+    def sum_1():
+        for half in range(2):
+            total = wc[half, firsts[half]].astype(F32)
+            for o in (1, 2, 3):
+                step1(half, o).wait_recv()
+                total = total + rx[half, o - 1].astype(F32)
+            wx[half] = total.astype(BF16)
+            for o in (1, 2, 3):
+                step2(half, o).start()
+
+    def sum_2():
+        for half in range(2):
+            total = wx[half, seconds[half]].astype(F32)
+            for o in (1, 2, 3):
+                step2(half, o).wait_recv()
+                total = total + rxy[half, o - 1].astype(F32)
+            total = total.astype(BF16)
+            for j in range(4):
+                wz[half * 4 + j] = total[:, j * HEAD : (j + 1) * HEAD]
         for o in range(1, 8):
             ar_z(o).start()
 
     def sum_z():
-        total = wy[z].astype(F32)
+        total = wz[z].astype(F32)
         for o in range(1, 8):
             ar_z(o).wait_recv()
             total = total + rz[o - 1].astype(F32)
@@ -353,21 +389,26 @@
     def gather_z():
         for o in range(1, 8):
             back_z(o).wait_recv()
-        for j in range(8):
-            gwf[core, x, y, :, j * HEAD : (j + 1) * HEAD] = fz[j]
-        for o in (1, 2, 3):
-            back_y(o).start()
-
-    def gather_y():
-        for o in (1, 2, 3):
-            back_y(o).wait_recv()
-        for o in (1, 2, 3):
-            back_x(o).start()
-
-    def gather_x():
-        for o in (1, 2, 3):
-            back_x(o).wait_recv()
-        back_core().start()
+        for half in range(2):
+            for j in range(4):
+                cols = slice(j * HEAD, (j + 1) * HEAD)
+                gwf[core, half, pl.ds(final_row(half), 16), cols] = fz[half * 4 + j]
+            for o in (1, 2, 3):
+                back2(half, o).start()
+
+    def gather_2():
+        for half in range(2):
+            for o in (1, 2, 3):
+                back2(half, o).wait_recv()
+            for o in (1, 2, 3):
+                back1(half, o).start()
+            back_core(half, 0).start()
+
+    def gather_1():
+        for half in range(2):
+            for o in (1, 2, 3):
+                back1(half, o).wait_recv()
+                back_core(half, o).start()
 
     def send_grad(a, k):
         return remote(
@@ -381,11 +422,12 @@
         def _():
             grad_home[a, head] = grad_send[a, 0]
 
-        @pl.when(k > 0)
-        def _():
-            send_grad(a, k).start()
-
     def query_block(k, carry):
+        @pl.when(k == 0)
+        def _():
+            for j in range(4):
+                spread_their(1, j)
+
         @pl.when(k == 2)
         def _():
             weight_term()
@@ -407,26 +449,32 @@
             ds = (p * (dot(grad, kv[other, 1], NT) - rd)).astype(BF16)
             acc = acc + dot(ds, keys, NN)
         give_grad(0, k, (acc * FACTOR).astype(BF16))
+
+        @pl.when(k > 0)
+        def _():
+            send_grad(0, k).start()
+
         return carry
 
     lax.fori_loop(0, 4, query_block, 0)
 
+    for m in range(CROSS):
+        spread_cross(1, m)
+    sum_1()
     all_here(1)
     for i in range(7):
         send_stats(i).wait_recv()
 
     def key_block(k, carry):
-        @pl.when(k == 0)
-        def _():
-            sum_x()
-
         @pl.when(k == 1)
         def _():
-            sum_y()
+            sum_2()
 
         @pl.when(k == 2)
         def _():
             sum_z()
+            for a in (1, 2):
+                send_grad(a, 1).start()
 
         @pl.when(k == 3)
         def _():
@@ -454,16 +502,15 @@
             acc_k = acc_k + dot(ds, query, NN)
         give_grad(1, k, (acc_k * FACTOR).astype(BF16))
         give_grad(2, k, acc_v.astype(BF16))
+
+        @pl.when(k >= 2)
+        def _():
+            for a in (1, 2):
+                send_grad(a, k).start()
+
         return carry
 
     lax.fori_loop(0, 4, key_block, 0)
-
-    gather_y()
-    projected = dot(out_home[0], w_ref[0:HEAD], NN)
-    for h in range(1, HEADS):
-        projected = projected + dot(out_home[h], w_ref[h * HEAD : (h + 1) * HEAD], NN)
-    proj_ref[...] = projected.astype(BF16)
-    gather_x()
 
     def home_grad(a, k):
         t = targets[k]
@@ -471,17 +518,42 @@
             grad_send.at[a, k], grad_home.at[a, t // 2], g_s.at[a, k], g_r.at[a, k], at(z_=t)
         )
 
-    for a, ref in enumerate((gq_ref, gk_ref, gv_ref)):
+    stores = []
+
+    def store(src, dst):
+        copy = pltpu.make_async_copy(src, dst, out_s.at[len(stores)])
+        copy.start()
+        stores.append(copy)
+
+    def finish(a, dst):
         for k in (1, 2, 3):
             home_grad(a, k).wait_recv()
         for h in range(HEADS):
-            ref[:, h * HEAD : (h + 1) * HEAD] = grad_home[a, h]
-    back_core().wait_recv()
-    for a in range(2):
-        for b in range(4):
-            for c in range(4):
-                row = a * 256 + b * 64 + c * 16
-                gw_ref[row : row + 16] = gwf[a, b, c]
+            store(grad_home.at[a, h], dst.at[:, pl.ds(h * HEAD, HEAD)])
+
+    gather_2()
+    projected = dot(out_home[0], w_ref[0:HEAD], NN)
+    for h in range(1, HEADS):
+        projected = projected + dot(out_home[h], w_ref[h * HEAD : (h + 1) * HEAD], NN)
+    proj_ref[...] = projected.astype(BF16)
+    store(proj_ref, proj_hbm)
+    finish(0, gq_hbm)
+    gather_1()
+    finish(1, gk_hbm)
+    finish(2, gv_hbm)
+
+    def store_weight(c):
+        for half in range(2):
+            rows, cols = pl.ds(pl.multiple_of(c * 256, 256), 256), pl.ds(half * 512, 512)
+            store(gwf.at[c, half], gw_hbm.at[rows, cols])
+
+    store_weight(core)
+    for half in range(2):
+        for o in range(4):
+            back_core(half, o).wait_recv()
+    store_weight(1 - core)
+    for copy in stores:
+        copy.wait()
 
     for k in (1, 2, 3):
         for kind in range(3):
@@ -501,56 +573,79 @@
         send_stats(i).wait_send()
     ar_core().wait_send()
     for o in (1, 2, 3):
-        for make in (ar_x, ar_y, back_y, back_x):
-            make(o).wait_send()
+        for half in range(2):
+            for make in (step1, step2, back2, back1):
+                make(half, o).wait_send()
     for o in range(1, 8):
         ar_z(o).wait_send()
         back_z(o).wait_send()
-    back_core().wait_send()
+    for half in range(2):
+        for o in range(4):
+            back_core(half, o).wait_send()
+
+
+def hand_on(*refs):
+    held, in_sems, out_sems = refs[10:15], refs[15], refs[16]
+    copies = []
+    for src, dst, mid in zip(refs[:5], refs[5:10], held):
+        rows = src.shape[0] // 2
+        for part in range(2):
+            piece, i = pl.ds(part * rows, rows), len(copies)
+            copies.append(
+                (
+                    pltpu.make_async_copy(src.at[piece], mid.at[piece], in_sems.at[i]),
+                    pltpu.make_async_copy(mid.at[piece], dst.at[piece], out_sems.at[i]),
+                )
+            )
+    for come, _ in copies:
+        come.start()
+    for come, go in copies:
+        come.wait()
+        go.start()
+    for _, go in copies:
+        go.wait()
 
 
 def on_device(query_rows, key_rows, value_rows, recordings, out_weight, cotangent):
-    labels = recordings[0]
-    start = jnp.sum(labels[None, :] < labels[:, None], axis=1).astype(jnp.int32)
-    count = jnp.sum(labels[None, :] == labels[:, None], axis=1).astype(jnp.int32)
-    vmem = pl.BlockSpec(memory_space=pltpu.VMEM)
+    vmem = pltpu.VMEM
     smem = pl.BlockSpec(memory_space=pltpu.SMEM)
+    hbm = pl.BlockSpec(memory_space=pl.ANY)
     dma = pltpu.SemaphoreType.DMA
-    outs = pl.pallas_call(
+    shapes = [(TOK, D), (TOK, ATT), (TOK, ATT), (TOK, ATT), (ATT, D)]
+    shapes = tuple(jax.ShapeDtypeStruct(shape, BF16) for shape in shapes)
+    results = pl.pallas_call(
         kernel,
-        out_shape=(
-            jax.ShapeDtypeStruct((TOK, D), BF16),
-            jax.ShapeDtypeStruct((TOK, ATT), BF16),
-            jax.ShapeDtypeStruct((TOK, ATT), BF16),
-            jax.ShapeDtypeStruct((TOK, ATT), BF16),
-            jax.ShapeDtypeStruct((ATT, D), BF16),
-        ),
-        in_specs=[smem, smem, vmem, vmem, vmem, vmem, vmem],
-        out_specs=(vmem,) * 5,
+        out_shape=shapes,
+        in_specs=[smem, hbm, hbm, hbm, hbm, hbm],
+        out_specs=(hbm,) * 5,
         scratch_shapes=[
-            pltpu.VMEM((WINDOW, 2, TOK, HEAD), BF16),
-            pltpu.VMEM((WINDOW, 2, TOK, HEAD), BF16),
-            pltpu.VMEM((HEADS, 2, TOK, HEAD), BF16),
-            pltpu.VMEM((HEADS, TOK, HEAD), BF16),
-            pltpu.VMEM((HEADS, TOK, HEAD), BF16),
-            pltpu.VMEM((8, 4, 16, TOK), F32),
-            pltpu.VMEM((4, TOK, HEAD), F32),
-            pltpu.VMEM((4, TOK, HEAD), F32),
-            pltpu.VMEM((MOST, TOK, TOK), F32),
-            pltpu.VMEM((4, TOK, HEAD), BF16),
-            pltpu.VMEM((HEADS, TOK, HEAD), BF16),
-            pltpu.VMEM((3, 4, TOK, HEAD), BF16),
-            pltpu.VMEM((3, HEADS, TOK, HEAD), BF16),
-            pltpu.VMEM((2, 4, 4, 16, D), BF16),
-            pltpu.VMEM((4, 4, 16, D), BF16),
-            pltpu.VMEM((4, 4, 16, D), BF16),
-            pltpu.VMEM((4, 16, D), BF16),
-            pltpu.VMEM((3, 4, 16, D), BF16),
-            pltpu.VMEM((8, 16, HEAD), BF16),
-            pltpu.VMEM((3, 16, D), BF16),
-            pltpu.VMEM((7, 16, HEAD), BF16),
-            pltpu.VMEM((8, 16, HEAD), BF16),
-            pltpu.VMEM((2, 4, 4, 16, D), BF16),
+            vmem((TOK, D), BF16),
+            vmem((ATT, D), BF16),
+            vmem((TOK, D), BF16),
+            pltpu.SMEM((2, 4), jnp.int32),
+            vmem((WINDOW, 2, TOK, HEAD), BF16),
+            vmem((WINDOW, 2, TOK, HEAD), BF16),
+            vmem((HEADS, 2, TOK, HEAD), BF16),
+            vmem((HEADS, TOK, HEAD), BF16),
+            vmem((HEADS, TOK, HEAD), BF16),
+            vmem((8, 4, 16, TOK), F32),
+            vmem((4, TOK, HEAD), F32),
+            vmem((4, TOK, HEAD), F32),
+            vmem((MOST, TOK, TOK), F32),
+            vmem((4, TOK, HEAD), BF16),
+            vmem((HEADS, TOK, HEAD), BF16),
+            vmem((3, 4, TOK, HEAD), BF16),
+            vmem((3, HEADS, TOK, HEAD), BF16),
+            vmem((2, 2, 4, 4, 16, 512), BF16),
+            vmem((2, 4, 4, 16, 512), BF16),
+            vmem((2, 4, 4, 16, 512), BF16),
+            vmem((2, 4, 16, 512), BF16),
+            vmem((2, 3, 4, 16, 512), BF16),
+            vmem((2, 3, 16, 512), BF16),
+            vmem((8, 16, HEAD), BF16),
+            vmem((7, 16, HEAD), BF16),
+            vmem((8, 16, HEAD), BF16),
+            vmem((2, 2, 256, 512), BF16),
         ]
         + [dma((3, 4))] * 2
         + [dma((2, 4))] * 6
@@ -558,13 +653,21 @@
         + [dma((7,))] * 2
         + [dma((4,))] * 2
         + [dma((3, 4))] * 2
-        + [dma((14,))] * 2
-        + [dma((2, 8))] * 2,
+        + [dma((5, 2, 4))] * 2
+        + [dma((2, 8))] * 2
+        + [dma((2, 4))] * 2
+        + [dma((14,)), dma((17,))],
         compiler_params=pltpu.CompilerParams(
             collective_id=0, has_side_effects=True, vmem_limit_bytes=56 << 20
         ),
-    )(start, count, query_rows[0], key_rows[0], value_rows[0], cotangent[0], out_weight)
-    projected, grad_query, grad_key, grad_value, grad_weight = outs
+    )(recordings, query_rows[0], key_rows[0], value_rows[0], cotangent[0], out_weight)
+    projected, grad_query, grad_key, grad_value, grad_weight = pl.pallas_call(
+        hand_on,
+        out_shape=shapes,
+        in_specs=[hbm] * 5,
+        out_specs=(hbm,) * 5,
+        scratch_shapes=[vmem(shape.shape, BF16) for shape in shapes] + [dma((10,))] * 2,
+    )(*results)
     return (projected[None], grad_query[None], grad_key[None], grad_value[None], grad_weight)
 
 

time: 117 us -> 99.9 us (0.85)
  Pallas kernels: 110 us -> 99.1 us
  local copies, waits for them, and re-layouts: 5.68 us -> 0 us
    pallas_call x1 -> x2, Pallas kernels: 110 us -> 99.1 us  [the longest x1 96.5 us: on_device(): pl.pallas_call(kernel, out_shape=shapes, in_specs=[smem, hbm, hbm, hbm, h...]
    unnamed x15 -> x0, local copies, waits for them, and re-layouts: 5.68 us -> none
where the time goes in v2:
time: 99.9 us; the launch traced here: 99.7 us
  Pallas kernels  99.1 us (99%)
    pallas_call x1, Pallas kernels, on_device(): pl.pallas_call(kernel, out_shape=shapes, in_specs=[smem, hbm, hbm, hbm, h...  96.5 us
    pallas_call x1, Pallas kernels, on_device(): pl.pallas_call(hand_on, out_shape=shapes, in_specs=[hbm] * 5, out_specs=(...  2.58 us

profile of v2, /device:TPU:1, one launch (start us, length us, event | category | flops | bytes accessed | tf_op | source)
XLA Modules:
  0.0 99.7 jit_solution(18207811475740266003)
XLA Ops:
  0.6 96.5 %shard_map.101 = (bf16[256,1024]{1,0:T(8,128)(2,1)}, bf16[256,512]{1,0:T(8,128)(2,1)}, bf16[256,512]{1,0:T(8,128)(2,1)}, bf16[256,512]{1,0:T(8,128)(2,1)}, bf16[512,1024]{1,0:T(8,128)(2,1)}) custom-call(s32[1,32]{1,0:T(1,128)} %rec_ref.1, bf16[256,512]{1,0:T(8,128)(2,1)} %bitcast.9, bf16[256,512]{1,0:T(8,128)(2,1)} %bitcast.10, bf16[256,512]{1,0:T(8,128)(2,1)} %bitcast.11, ...), custom_call_target="tpu_custom_call" | custom-call | tf_op jit(solution)/shard_map/pallas_call | solution.py:616
  97.2 2.6 %shard_map.102 = (bf16[256,1024]{1,0:T(8,128)(2,1)}, bf16[256,512]{1,0:T(8,128)(2,1)}, bf16[256,512]{1,0:T(8,128)(2,1)}, bf16[256,512]{1,0:T(8,128)(2,1)}, bf16[512,1024]{1,0:T(8,128)(2,1)}) custom-call(bf16[256,1024]{1,0:T(8,128)(2,1)} %get-tuple-element.15.refs_0_, bf16[256,512]{1,0:T(8,128)(2,1)} %get-tuple-element.16.refs_1_, ...), custom_call_target="tpu_custom_call" | custom-call | tf_op jit(solution)/shard_map/pallas_call | solution.py:664

commit v3 on v2

--- a/solution.py
+++ b/solution.py
@@ -234,6 +234,11 @@
         return jnp.where(t < count, 0.0, FAR)
 
     def forward_block(k, carry):
+        @pl.when(k == 3)
+        def _():
+            for j in range(4):
+                spread_their(1, j)
+
         sl = slot(own_z(k), core)
         first, count = block_range(k)
         query = qd[sl, 0]
@@ -423,11 +428,6 @@
             grad_home[a, head] = grad_send[a, 0]
 
     def query_block(k, carry):
-        @pl.when(k == 0)
-        def _():
-            for j in range(4):
-                spread_their(1, j)
-
         @pl.when(k == 2)
         def _():
             weight_term()
@@ -458,25 +458,20 @@
 
     lax.fori_loop(0, 4, query_block, 0)
 
+    sum_1()
     for m in range(CROSS):
         spread_cross(1, m)
-    sum_1()
     all_here(1)
+    sum_2()
     for i in range(7):
         send_stats(i).wait_recv()
 
     def key_block(k, carry):
         @pl.when(k == 1)
         def _():
-            sum_2()
+            sum_z()
 
         @pl.when(k == 2)
-        def _():
-            sum_z()
-            for a in (1, 2):
-                send_grad(a, 1).start()
-
-        @pl.when(k == 3)
         def _():
             gather_z()
 
@@ -503,7 +498,7 @@
         give_grad(1, k, (acc_k * FACTOR).astype(BF16))
         give_grad(2, k, acc_v.astype(BF16))
 
-        @pl.when(k >= 2)
+        @pl.when(k >= 1)
         def _():
             for a in (1, 2):
                 send_grad(a, k).start()

time: 99.9 us -> 98.2 us (0.983)
  Pallas kernels: 99.1 us -> 97.4 us
    pallas_call x1, Pallas kernels: 96.5 us -> 94.8 us  [on_device(): pl.pallas_call(kernel, out_shape=shapes, in_specs=[smem, hbm, hbm, hbm, h...]
where the time goes in v3:
time: 98.2 us; the launch traced here: 98 us
  Pallas kernels  97.4 us (99%)
    pallas_call x1, Pallas kernels, on_device(): pl.pallas_call(kernel, out_shape=shapes, in_specs=[smem, hbm, hbm, hbm, h...  94.8 us
    pallas_call x1, Pallas kernels, on_device(): pl.pallas_call(hand_on, out_shape=shapes, in_specs=[hbm] * 5, out_specs=(...  2.58 us

profile of v3, /device:TPU:1, one launch (start us, length us, event | category | flops | bytes accessed | tf_op | source)
XLA Modules:
  0.0 98.0 jit_solution(15168883792727066057)
XLA Ops:
  0.6 94.8 %shard_map.101 = (bf16[256,1024]{1,0:T(8,128)(2,1)}, bf16[256,512]{1,0:T(8,128)(2,1)}, bf16[256,512]{1,0:T(8,128)(2,1)}, bf16[256,512]{1,0:T(8,128)(2,1)}, bf16[512,1024]{1,0:T(8,128)(2,1)}) custom-call(s32[1,32]{1,0:T(1,128)} %rec_ref.1, bf16[256,512]{1,0:T(8,128)(2,1)} %bitcast.9, bf16[256,512]{1,0:T(8,128)(2,1)} %bitcast.10, bf16[256,512]{1,0:T(8,128)(2,1)} %bitcast.11, ...), custom_call_target="tpu_custom_call" | custom-call | tf_op jit(solution)/shard_map/pallas_call | solution.py:611
  95.4 2.6 %shard_map.102 = (bf16[256,1024]{1,0:T(8,128)(2,1)}, bf16[256,512]{1,0:T(8,128)(2,1)}, bf16[256,512]{1,0:T(8,128)(2,1)}, bf16[256,512]{1,0:T(8,128)(2,1)}, bf16[512,1024]{1,0:T(8,128)(2,1)}) custom-call(bf16[256,1024]{1,0:T(8,128)(2,1)} %get-tuple-element.15.refs_0_, bf16[256,512]{1,0:T(8,128)(2,1)} %get-tuple-element.16.refs_1_, ...), custom_call_target="tpu_custom_call" | custom-call | tf_op jit(solution)/shard_map/pallas_call | solution.py:659

commit v4 on v3

--- a/solution.py
+++ b/solution.py
@@ -534,8 +534,6 @@
     store(proj_ref, proj_hbm)
     finish(0, gq_hbm)
     gather_1()
-    finish(1, gk_hbm)
-    finish(2, gv_hbm)
 
     def store_weight(c):
         for half in range(2):
@@ -543,6 +541,8 @@
             store(gwf.at[c, half], gw_hbm.at[rows, cols])
 
     store_weight(core)
+    finish(1, gk_hbm)
+    finish(2, gv_hbm)
     for half in range(2):
         for o in range(4):
             back_core(half, o).wait_recv()

time: 98.2 us -> 98.2 us (level)
  no operation moved by 1% of the time
where the time goes in v4:
time: 98.2 us; the launch traced here: 98 us
  Pallas kernels  97.4 us (99%)
    pallas_call x1, Pallas kernels, on_device(): pl.pallas_call(kernel, out_shape=shapes, in_specs=[smem, hbm, hbm, hbm, h...  94.8 us
    pallas_call x1, Pallas kernels, on_device(): pl.pallas_call(hand_on, out_shape=shapes, in_specs=[hbm] * 5, out_specs=(...  2.58 us

profile of v4, /device:TPU:1, one launch (start us, length us, event | category | flops | bytes accessed | tf_op | source)
XLA Modules:
  0.0 98.0 jit_solution(3034183676552455413)
XLA Ops:
  0.6 94.8 %shard_map.101 = (bf16[256,1024]{1,0:T(8,128)(2,1)}, bf16[256,512]{1,0:T(8,128)(2,1)}, bf16[256,512]{1,0:T(8,128)(2,1)}, bf16[256,512]{1,0:T(8,128)(2,1)}, bf16[512,1024]{1,0:T(8,128)(2,1)}) custom-call(s32[1,32]{1,0:T(1,128)} %rec_ref.1, bf16[256,512]{1,0:T(8,128)(2,1)} %bitcast.9, bf16[256,512]{1,0:T(8,128)(2,1)} %bitcast.10, bf16[256,512]{1,0:T(8,128)(2,1)} %bitcast.11, ...), custom_call_target="tpu_custom_call" | custom-call | tf_op jit(solution)/shard_map/pallas_call | solution.py:611
  95.4 2.6 %shard_map.102 = (bf16[256,1024]{1,0:T(8,128)(2,1)}, bf16[256,512]{1,0:T(8,128)(2,1)}, bf16[256,512]{1,0:T(8,128)(2,1)}, bf16[256,512]{1,0:T(8,128)(2,1)}, bf16[512,1024]{1,0:T(8,128)(2,1)}) custom-call(bf16[256,1024]{1,0:T(8,128)(2,1)} %get-tuple-element.15.refs_0_, bf16[256,512]{1,0:T(8,128)(2,1)} %get-tuple-element.16.refs_1_, ...), custom_call_target="tpu_custom_call" | custom-call | tf_op jit(solution)/shard_map/pallas_call | solution.py:659
